TPU v7x, 256 devices: a whole 4x4x8 slice. The times are simulated.
256 devices in a mesh: rep: 4 (over z_lo), fsdp: 64 (over y, x, z_hi, core).
Axes of the slice: x: 4, y: 4, z: 8 (z_hi: 2, z_lo: 4; z = z_hi * 4 + z_lo), core: 2. Of those that a mesh axis runs over, the one named last changes fastest.
Arguments:
- step_index: int32 [1], replicated, may hold values from 0 to 63
- tokens: bfloat16 [4, 32768, 2304], P('rep', 'fsdp'), may hold values from -16 to 16
- queries: bfloat16 [4, 32768, 2048], P('rep', 'fsdp'), may hold values from -128 to 128
- cotangent: bfloat16 [4, 32768, 2048], P('rep', 'fsdp'), may hold values from -6 to 6
- params: float32 [4, 2304, 2048], P('rep', 'fsdp'), may hold values from -6 to 6
- momentum: float32 [4, 2304, 2048], P('rep', 'fsdp'), may hold values from -6 to 6
Outputs:
- new_params: float32 [4, 2304, 2048], P('rep', 'fsdp')
- new_moments: float32 [4, 2304, 2048], P('rep', 'fsdp')
All inputs are finite; a program needn't handle non-finite values.
Results may differ from a plain program's by a relative error of at most 0.006.
The roundings to bfloat16 on the way count: a program that leaves them out, or rounds other values in their place, can miss the bound.
Values may be sent and summed in bfloat16 or wider, within the bound.
A program may use at most 128 MiB of HBM per device.

v0:
```python
import jax
import jax.numpy as jnp
from jax import lax
from jax.sharding import PartitionSpec as P

QH = 16
KVH = 8
HEAD = 128
LENGTH = 256


SOFT_CAP = 50.0
SCORE_SCALE = 144.0 ** (-0.5)
ROPE_THETA = 10000.0
LEARN_RATE = 0.1
WARM_SPAN = 64.0
MOMENTUM_DECAY = 0.9


def from_behind(block, axis, distance):
    devices = range(lax.axis_size(axis))
    route = [((i - distance) % len(devices), i) for i in devices]
    return lax.ppermute(block, axis, route)


def rope_tables():
    half_head = HEAD // 2
    inverse = ROPE_THETA ** (-jnp.arange(half_head, dtype=jnp.float32) / half_head)
    angles = jnp.arange(LENGTH, dtype=jnp.float32)[:, None] * inverse[None, :]
    return (jnp.cos(angles), jnp.sin(angles))


def make_term(tok_rows, grad_cols):
    return lax.dot_general(
        tok_rows, grad_cols, (((0,), (0,)), ((), ())), preferred_element_type=jnp.float32
    )


def pull_state(stacked, phase_index, levels):

    def fetcher(distance):

        def fetch_state(payload):
            return from_behind(payload, "rep", distance)

        return fetch_state

    return lax.switch(phase_index, [fetcher(1 << level) for level in range(levels)], stacked)


def shards(step_index, tokens, queries, cotangent, params, momentum):
    tok_rows = tokens[0]
    tok_count, model_width = tok_rows.shape
    sequences = tok_count // LENGTH
    scale_in = model_width ** (-0.5)
    groups = QH // KVH
    half_head = HEAD // 2
    key_width = KVH * HEAD
    levels = lax.axis_size("rep").bit_length() - 1
    phase_index = step_index[0] % levels
    learn_now = LEARN_RATE * (step_index[0].astype(jnp.float32) + 1.0) / WARM_SPAN
    own_params = params[0]
    own_moments = momentum[0]
    weight_shard = own_params.astype(jnp.bfloat16)
    summed = jnp.dot(
        tok_rows,
        lax.all_gather(weight_shard, "fsdp", axis=0, tiled=True),
        preferred_element_type=jnp.float32,
    )
    joined = (summed * scale_in).astype(jnp.bfloat16)
    key_heads = joined[:, :key_width].astype(jnp.float32).reshape(sequences, LENGTH, KVH, HEAD)
    value_low = joined[:, key_width:].reshape(sequences, LENGTH, KVH, HEAD)
    query_low = queries[0].reshape(sequences, LENGTH, KVH, groups, HEAD)
    upstream_low = cotangent[0].reshape(sequences, LENGTH, KVH, groups, HEAD)
    cosine, sine_table = rope_tables()
    cos_rows = cosine[None, :, None, :]
    sin_rows = sine_table[None, :, None, :]
    lower = key_heads[..., :half_head]
    upper = key_heads[..., half_head:]
    rotated_low = jnp.concatenate(
        [lower * cos_rows - upper * sin_rows, upper * cos_rows + lower * sin_rows], axis=-1
    ).astype(jnp.bfloat16)
    scores = (
        jnp.einsum("bqngd,bknd->bngqk", query_low, rotated_low, preferred_element_type=jnp.float32)
        * SCORE_SCALE
    )
    bent = jnp.tanh(scores / SOFT_CAP)
    causal = lax.broadcasted_iota(jnp.int32, (LENGTH, LENGTH), 0) >= lax.broadcasted_iota(
        jnp.int32, (LENGTH, LENGTH), 1
    )
    weights = jnp.where(causal, jnp.exp(SOFT_CAP * bent), 0.0)
    shares = weights / jnp.sum(weights, axis=-1, keepdims=True)
    shares_low = shares.astype(jnp.bfloat16)
    value_grad = jnp.einsum(
        "bngqk,bqngd->bknd", shares_low, upstream_low, preferred_element_type=jnp.float32
    )
    share_grad = jnp.einsum(
        "bqngd,bknd->bngqk", upstream_low, value_low, preferred_element_type=jnp.float32
    )
    capped_grad = shares * (share_grad - jnp.sum(shares * share_grad, axis=-1, keepdims=True))
    score_low = (capped_grad * (1.0 - bent * bent) * SCORE_SCALE).astype(jnp.bfloat16)
    rotated_grad = jnp.einsum(
        "bngqk,bqngd->bknd", score_low, query_low, preferred_element_type=jnp.float32
    )
    lower_grad = rotated_grad[..., :half_head]
    upper_grad = rotated_grad[..., half_head:]
    unrotated = jnp.concatenate(
        [
            lower_grad * cos_rows + upper_grad * sin_rows,
            upper_grad * cos_rows - lower_grad * sin_rows,
        ],
        axis=-1,
    )
    both_grads = (
        jnp.concatenate(
            [unrotated.reshape(tok_count, key_width), value_grad.reshape(tok_count, key_width)],
            axis=1,
        )
        * scale_in
    ).astype(jnp.bfloat16)
    gradient = lax.psum_scatter(
        make_term(tok_rows, both_grads), "fsdp", scatter_dimension=0, tiled=True
    )
    moment = MOMENTUM_DECAY * own_moments + gradient
    stepped = own_params - learn_now * moment
    peer_state = pull_state(jnp.stack([stepped, moment]), phase_index, levels)
    new_params = 0.5 * (stepped + peer_state[0])
    new_moments = 0.5 * (moment + peer_state[1])
    return (new_params[None], new_moments[None])


def solution(mesh):
    return jax.shard_map(
        shards,
        mesh=mesh,
        in_specs=(
            P(),
            P("rep", "fsdp", None),
            P("rep", "fsdp", None),
            P("rep", "fsdp", None),
            P("rep", "fsdp", None),
            P("rep", "fsdp", None),
        ),
        out_specs=(P("rep", "fsdp", None), P("rep", "fsdp", None)),
        check_vma=False,
    )
```

profile of v0, /device:TPU:1, one launch (start us, length us, event | category | flops | bytes accessed | tf_op | source)
XLA Modules:
  0.0 1294.7 jit_solution(7300788189090091316)
XLA Ops:
  7.2 0.0 copy-start
  7.2 0.0 all-gather.3.cloned.1.call-start
  7.2 1.9 copy.125
  9.1 0.0 all-gather.3.cloned.1.call-update
  9.1 0.0 all-reduce.3.cloned.1.call-start
  9.2 4.4 reshape_squeeze.6
  13.6 6.1 copy.54
  19.7 4.5 reshape_squeeze.7
  24.2 0.5 fusion.39
  24.7 115.1 %all-gather.3.cloned.1.call-done = bf16[64,36,2048]{2,1,0:T(8,128)(2,1)} async-done(((bf16[1,36,2048]{2,1,0:T(8,128)(2,1)}), bf16[64,36,2048]{2,1,0:T(8,128)(2,1)}) %all-gather.3.cloned.1.call-update) | async-done | bytes 9437200 | tf_op jit(solution)/shard_map/all_gather | solution.py:67
  139.8 13.1 %reshape.77 = bf16[2304,2048]{1,0:T(8,128)(2,1)} reshape(bf16[64,36,2048]{2,1,0:T(8,128)(2,1)} %all-gather.3.cloned.1.call-done) | data formatting | bytes 18874368
  152.9 0.0 copy-done
  152.9 8.9 multiply_convert_fusion
  161.8 0.4 slice_bitcast_fusion
  162.3 0.5 copy.81
  162.8 0.7 fusion.51
  163.4 0.0 copy-start.1
  163.4 0.3 copy.82
  163.7 0.1 bitcast_bitcast_fusion
  163.8 1.2 copy-done.1
  165.0 4.5 fusion.17
  169.5 0.0 copy-start.3
  169.5 0.8 subtract_convert_fusion
  170.3 0.8 copy-done.3
  171.1 2.9 fusion.5
  174.0 0.0 copy-start.6
  174.1 3.2 copy-done.6
  177.3 4.1 fusion.22
  181.3 18.8 %fusion.19 = f32[2,256,8,128]{3,1,2,0:T(8,128)} fusion(bf16[2,256,8,2,128]{1,4,3,2,0:T(8,128)(2,1)} %copy.54, f32[2,8,256,256,2]{3,2,4,1,0:T(8,128)} %fusion.17, f32[2,8,256,256,2]{3,2,4,1,0:T(8,128)} %copy-done.6, f32[2,8,2,256]{3,2,1,0:T(2,128)S(1)} %get-tuple-element.29, pred[256,256]{0,1:T(8,128)(4,1)S(1)} %iota_compare_fusion), kind=kOutput, calls=%fused_computation.33 | convolution fusion | flops 570433792 | bytes 21069824 | tf_op jit(solution)/shard_map/bngqk,bqngd->bknd/dot_general | solution.py:102
  200.1 2.9 multiply_add_fusion
  203.0 0.6 pad_maximum_fusion
  203.6 0.0 copy-start.4
  203.7 1.2 copy.56
  204.9 0.4 copy-done.4
  205.2 1.2 copy.58
  206.5 1.0 copy_bitcast_fusion
  207.5 9.4 convolution_bitcast_fusion
  216.8 0.0 copy-start.5
  216.8 0.0 all-reduce.3.cloned.1.call-update
  217.5 0.0 copy-done.5
  217.5 0.6 dynamic-slice
  218.8 1032.7 %all-reduce.3.cloned.1.call-done = f32[2304,2048]{0,1:T(8,128)} async-done(((f32[2304,2048]{0,1:T(8,128)}), f32[2304,2048]{0,1:T(8,128)}) %all-reduce.3.cloned.1.call-update) | async-done | bytes 18874384
  1251.5 1.9 constant_dynamic-slice_fusion
  1253.5 1.1 copy.59
  1254.5 0.0 copy-start.2
  1254.5 1.4 fusion.40
  1255.9 0.3 copy.60
  1256.2 0.3 copy.61
  1256.6 0.5 pad_maximum_fusion.1
  1257.1 26.4 %conditional.1 = (f32[2,36,2048]{2,0,1:T(2,128)}) conditional(s32[]{:T(128)} %clamp.3, f32[2,36,2048]{2,0,1:T(2,128)S(1)} %pad_maximum_fusion.1, f32[2,36,2048]{2,0,1:T(2,128)S(1)} %pad_maximum_fusion.1), branch_computations={%region_3.4_spmd, %region_4.5_spmd} | conditional | bytes 2359344 | solution.py:48
  1257.1 2.9 collective-permute-start.1
  1260.0 23.5 %collective-permute-done.1 = f32[2,36,2048]{2,0,1:T(2,128)} collective-permute-done((f32[2,36,2048]{2,0,1:T(2,128)S(1)}, f32[2,36,2048]{2,0,1:T(2,128)}, u32[]{:S(2)}, u32[]{:S(2)}) %collective-permute-start.1) | collective-permute-done | bytes 589856 | tf_op jit(solution)/shard_map/cond/branch_1_fun/ppermute | solution.py:23
  1283.5 1.9 fusion.52
  1285.4 0.0 copy-done.2
  1285.4 0.4 fusion.33
  1285.8 1.0 copy.64
  1286.8 1.0 copy.65
  (2 shorter events, 0.0 us)
Async XLA Ops:
  7.2 145.7 %copy-start = (bf16[1,512,2304]{2,1,0:T(8,128)(2,1)S(1)}, bf16[1,512,2304]{2,1,0:T(8,128)(2,1)}, u32[]{:S(2)}) copy-start(bf16[1,512,2304]{2,1,0:T(8,128)(2,1)} %param.9) | copy-start | bytes 7077892
  7.2 132.6 %all-gather.3.cloned.1.call-start = ((), (), s32[]{:S(2)}) async-start(), calls=%async_computation | async-start | bytes 10649600 | tf_op jit(solution)/shard_map/all_gather | solution.py:67
  9.1 1242.4 %all-reduce.3.cloned.1.call-start = ((), (), s32[]{:S(2)}) async-start(), calls=%async_computation.1 | async-start | bytes 37748736
  163.4 1.6 copy-start.1
  169.5 1.6 copy-start.3
  174.0 3.2 copy-start.6
  203.6 1.6 copy-start.4
  216.8 0.7 copy-start.5
  1254.5 30.9 %copy-start.2 = (f32[1,36,2048]{2,0,1:T(1,128)S(1)}, f32[1,36,2048]{2,0,1:T(1,128)}, u32[]{:S(2)}) copy-start(f32[1,36,2048]{2,0,1:T(1,128)} %param.12) | copy-start | bytes 884740
  1257.1 26.4 %collective-permute-start.1 = (f32[2,36,2048]{2,0,1:T(2,128)S(1)}, f32[2,36,2048]{2,0,1:T(2,128)}, u32[]{:S(2)}, u32[]{:S(2)}) collective-permute-start(f32[2,36,2048]{2,0,1:T(2,128)S(1)} %param.1), channel_id=1, source_target_pairs={{128,0},{192,64},{0,128},{64,192},{129,1},{193,65},{1,129},{65,193... | collective-permute-start | bytes 1769480 | tf_op jit(solution)/shard_map/cond/branch_1_fun/ppermute | solution.py:23
Sparse Core Ops, SparseCore 0:
  12.1 127.6 all-gather.2
  217.0 1034.4 all-reduce.2
where the time goes:
time: 1300 us; the launch traced here: 1290 us
  waiting for transfers between devices  1170 us (90%)
  local copies, waits for them, and re-layouts  48.6 us (4%)
  matrix products  48.6 us (4%)
  between operations  15.6 us (1%)
    unnamed x3, waiting for transfers between devices  1030 us
    all_gather x1, waiting for transfers between devices, shards(): lax.all_gather(weight_shard, 'fsdp', axis=0, tiled=True)  115 us
  transfers between devices with their start and end apart: 3, of which 3 were waited for; matrix products, arithmetic and copies ran while one was open for 1% of the time, Pallas kernels for 0%

commit v1 on v0

v1 whole, which is shorter than its diff:
```python
import functools

import jax
import jax.numpy as jnp
import numpy as np
from jax import lax
from jax.experimental import pallas as pl
from jax.experimental.pallas import tpu as pltpu
from jax.sharding import PartitionSpec as P

MESH = pl.DeviceIdType.MESH
F32 = jnp.float32
BF16 = jnp.bfloat16

HEAD = 128
LENGTH = 256
SOFT_CAP = 50.0
SCORE_SCALE = 144.0 ** (-0.5)
ROPE_THETA = 10000.0
LEARN_RATE = 0.1
WARM_SPAN = 64.0
MOMENTUM_DECAY = 0.9

D = 2304
TOK = 512
CH = 4
ROWS = 144
OWN = 36
WIDE = 2048

M_QUAD = 0
M_AG = 3
M_RS = 19
M_Z = 43
M_FIX = 44
M_GOS = 45
M_ALL = 49


def rope_tables():
    half = HEAD // 2
    inverse = np.float32(ROPE_THETA) ** (-np.arange(half, dtype=np.float32) / np.float32(half))
    angles = np.arange(LENGTH, dtype=np.float32)[:, None] * inverse[None, :].astype(np.float32)
    cos, sin = np.cos(angles), np.sin(angles)
    cos_full = np.concatenate([cos, cos], axis=1).astype(np.float32)
    sin_signed = np.concatenate([-sin, sin], axis=1).astype(np.float32)
    return cos_full, sin_signed


def m16(value, by=16):
    return pl.multiple_of(value, by)


SCRATCH = dict(
    tok=((2 * TOK, D), BF16),
    tok_t=((D, 2 * TOK), BF16),
    q=((2 * TOK, 1024), BF16),
    cot=((2 * TOK, 1024), BF16),
    p=((OWN, WIDE), F32),
    m=((OWN, WIDE), F32),
    peer=((2, 2, OWN, WIDE), F32),
    piece=((CH, 2, 48, 256), BF16),
    pin=((CH, 4, 48, 256), BF16),
    w=((CH, 4, 576, 256), BF16),
    grads=((2 * TOK, 256), BF16),
    f=((CH, 4, 576, 256), F32),
    g=((CH, 4, 576, 256), BF16),
    h=((CH, 2, 4, ROWS, 128), F32),
    hb=((CH, 2, 4, ROWS, 128), BF16),
    e=((CH, ROWS, 256), F32),
    zs=((CH, 80, 256), BF16),
    zr=((CH, 80, 256), BF16),
    fs=((CH, 40, 256), F32),
    gx=((CH, 2, 40, 256), F32),
    gb=((CH, 2, 48, 256), BF16),
    gp=((2, CH, 2, 48, 256), BF16),
)
PARTS = ("al", "bl", "cl", "ar", "br", "cr", "tr", "tl")
P_PARTS = ("al", "cl", "br", "tr")
for _name in PARTS:
    SCRATCH["x0" + _name] = ((CH, 2, ROWS, 128), BF16)
    SCRATCH["x1" + _name] = ((CH, 288, 128), BF16)
    for _half in (0, 1):
        SCRATCH["y%d%s" % (_half, _name)] = ((CH, 80 if _name in P_PARTS else 64, 128), BF16)
NAMES = tuple(SCRATCH)


def kernel(step_ref, tok_h, q_h, cot_h, p_h, m_h, cos_ref, sin_ref, outp_ref, outm_ref, *scratch):
    b = dict(zip(NAMES, scratch))
    ssem, rsem, gssem, grsem, lsem = scratch[len(NAMES):]
    rep = lax.axis_index("rep")
    f = lax.axis_index("fsdp")
    core = lax.rem(f, 2)
    zh = lax.rem(f // 2, 2)
    x = lax.rem(f // 4, 4)
    y = f // 16
    other = 1 - core

    def dev(r=rep, yy=y, xx=x, zz=zh, cc=core):
        return (r, ((yy * 4 + xx) * 2 + zz) * 2 + cc)

    def up(i, by=1):
        return lax.rem(i + by, 4)

    side = {
        "x": dict(me=x, r=dev(xx=up(x)), l=dev(xx=up(x, 3))),
        "y": dict(me=y, r=dev(yy=up(y)), l=dev(yy=up(y, 3))),
    }

    def axis_of(half, phase):
        return side["x" if half == phase else "y"]

    def axis_rs(half, phase):
        return side["x" if half == phase else "y"]

    def rc(src, dst, c, k, where):
        return pltpu.make_async_remote_copy(
            src_ref=src, dst_ref=dst, send_sem=ssem.at[c, k], recv_sem=rsem.at[c, k],
            device_id=where, device_id_type=MESH)

    my_rows = pl.ds(m16(core * TOK, TOK), TOK)
    my_cols = pl.ds(m16(core * 1024, 1024), 1024)
    other_cols = pl.ds(m16(other * 1024, 1024), 1024)
    loads = [
        pltpu.make_async_copy(p_h.at[0], b["p"], lsem.at[0]),
        pltpu.make_async_copy(m_h.at[0], b["m"], lsem.at[1]),
        pltpu.make_async_copy(tok_h.at[0], b["tok"].at[my_rows, :], lsem.at[2]),
        pltpu.make_async_copy(q_h.at[0, :, my_cols], b["q"].at[my_rows, :], lsem.at[3]),
        pltpu.make_async_copy(cot_h.at[0, :, my_cols], b["cot"].at[my_rows, :], lsem.at[4]),
    ]
    for load in loads:
        load.start()

    barrier = pltpu.get_barrier_semaphore()
    partners = [dev(cc=other), dev(zz=1 - zh), dev(zz=1 - zh, cc=other)]
    partners += [side[a][d] for a in ("x", "y") for d in ("r", "l")]
    partners += [dev(r=up(rep, d), cc=cc) for d in (1, 2, 3) for cc in (core, other)]
    for partner in partners:
        pl.semaphore_signal(barrier, inc=1, device_id=partner, device_id_type=MESH)

    loads[0].wait()
    for c in range(CH):
        for d in range(2):
            k0 = d * 512 + c * 128
            v = jnp.concatenate([b["p"][:, k0:k0 + 128], b["p"][:, 1024 + k0:1024 + k0 + 128]], axis=1)
            v = jnp.concatenate([v, jnp.zeros((12, 256), F32)], axis=0)
            b["piece"][c, d] = v.astype(BF16)

    pl.semaphore_wait(barrier, len(partners))

    quad = [(dev(cc=other), zh * 2 + other, other),
            (dev(zz=1 - zh), (1 - zh) * 2 + core, core),
            (dev(zz=1 - zh, cc=other), (1 - zh) * 2 + other, other)]
    my_slot = zh * 2 + core

    def quad_send(c):
        for k, (where, _, d) in enumerate(quad):
            rc(b["piece"].at[c, d], b["pin"].at[c, my_slot], c, M_QUAD + k, where).start()

    def quad_done(c):
        for k, (where, slot, d) in enumerate(quad):
            rc(b["piece"].at[c, d], b["pin"].at[c, slot], c, M_QUAD + k, where).wait_recv()
        b["pin"][c, my_slot] = b["piece"][c, core]
        v = [b["pin"][c, s].astype(F32)[:OWN] for s in range(4)]
        b["w"][c, y, pl.ds(m16(x * ROWS), ROWS), :] = jnp.concatenate(v, axis=0).astype(BF16)

    def w_unit(c, half, phase, j, part):
        lanes = pl.ds(half * 128, 128)
        w = b["w"]
        if phase == 0:
            at, n = dict(all=(0, ROWS), p=(0, 80), q=(80, 64))[part]
            if half == 0:
                return w.at[c, y, pl.ds(m16(j * ROWS + at), n), lanes]
            return w.at[c, j, pl.ds(m16(x * ROWS + at), n), lanes]
        if half == 0:
            at, n = dict(all=(0, 576), p=(0, 288), q=(288, 288))[part]
            return w.at[c, j, pl.ds(at, n), lanes]
        at, n = dict(all=(0, 4), p=(0, 2), q=(2, 2))[part]
        return w.at[c, pl.ds(at, n), pl.ds(m16(j * ROWS), ROWS), lanes]

    def ag_copy(c, half, phase, k, j):
        s = axis_of(half, phase)
        unit = w_unit(c, half, phase, j, ("all", "all", "p", "q")[k])
        return rc(unit, unit, c, M_AG + half * 8 + phase * 4 + k, s["r"] if k % 2 == 0 else s["l"])

    def ag_start(c, half, phase):
        me = axis_of(half, phase)["me"]
        ag_copy(c, half, phase, 0, me).start()
        ag_copy(c, half, phase, 1, me).start()

    def ag_mid(c, half, phase):
        me = axis_of(half, phase)["me"]
        ag_copy(c, half, phase, 0, up(me, 3)).wait_recv()
        ag_copy(c, half, phase, 2, up(me, 3)).start()
        ag_copy(c, half, phase, 1, up(me)).wait_recv()
        ag_copy(c, half, phase, 3, up(me)).start()

    def ag_end(c, half, phase):
        me = axis_of(half, phase)["me"]
        ag_copy(c, half, phase, 2, up(me, 2)).wait_recv()
        ag_copy(c, half, phase, 3, up(me, 2)).wait_recv()

    def transpose_rows(s):
        rows = pl.ds(m16(s * 256, 256), 256)

        def one(k, _):
            cols = pl.ds(m16(k * 256, 256), 256)
            b["tok_t"][cols, rows] = b["tok"][rows, cols].T
            return 0

        lax.fori_loop(0, D // 256, one, 0)

    causal = lax.broadcasted_iota(jnp.int32, (LENGTH, LENGTH), 0) <= lax.broadcasted_iota(
        jnp.int32, (LENGTH, LENGTH), 1)
    scale_in = D ** (-0.5)

    def nt(a, bb):
        return lax.dot_general(a, bb, (((1,), (1,)), ((), ())), preferred_element_type=F32)

    def attend(c, s):
        rows = pl.ds(m16(s * 256, 256), 256)
        w = b["w"][c].reshape(D, 256)
        joined = (jnp.dot(b["tok"][rows, :], w, preferred_element_type=F32) * scale_in).astype(BF16)
        key = joined[:, :HEAD].astype(F32)
        val = joined[:, HEAD:]
        cos, sin = cos_ref[...], sin_ref[...]
        rot = (key * cos + pltpu.roll(key, 64, 1) * sin).astype(BF16)
        d_val = jnp.zeros((LENGTH, HEAD), F32)
        d_rot = jnp.zeros((LENGTH, HEAD), F32)
        for head in range(2):
            cols = pl.ds(m16(c * 256 + head * 128, 128), 128)
            qh = b["q"][rows, cols]
            ch = b["cot"][rows, cols]
            bent = jnp.tanh(nt(rot, qh) * (SCORE_SCALE / SOFT_CAP))
            weights = jnp.where(causal, jnp.exp(SOFT_CAP * bent), 0.0)
            shares = weights * (1.0 / jnp.sum(weights, axis=0, keepdims=True))
            d_val += jnp.dot(shares.astype(BF16), ch, preferred_element_type=F32)
            share_grad = nt(val, ch)
            mean = jnp.sum(shares * share_grad, axis=0, keepdims=True)
            score = shares * (share_grad - mean) * ((1.0 - bent * bent) * SCORE_SCALE)
            d_rot += jnp.dot(score.astype(BF16), qh, preferred_element_type=F32)
        d_key = d_rot * cos - pltpu.roll(d_rot, 64, 1) * sin
        b["grads"][rows, :] = (jnp.concatenate([d_key, d_val], axis=1) * scale_in).astype(BF16)

    def gradient(c, yy):
        rows = pl.ds(m16(yy * 576, 64), 576)
        v = jnp.dot(b["tok_t"][rows, :], b["grads"][...], preferred_element_type=F32)
        b["f"][c, yy] = v
        b["g"][c, yy] = v.astype(BF16)

    def unit(name, c, half, phase, j, part):
        if phase == 0:
            ref = b["f" if name == "f" else "g"]
            if half == 0:
                return ref.at[c, pl.ds(0 if part == "p" else 2, 2), pl.ds(m16(j * ROWS), ROWS), pl.ds(0, 128)]
            return ref.at[c, j, pl.ds(0 if part == "p" else 288, 288), pl.ds(128, 128)]
        ref = b["h" if name == "f" else "hb"]
        return ref.at[c, half, j, pl.ds(0, 80) if part == "p" else pl.ds(80, 64), :]

    def buf(c, half, phase, name):
        return b["xy"[phase] + str(half) + name].at[c]

    RS_DST = ("al", "ar", "bl", "br", "cl", "cr")
    RS_PART = ("p", "q", "q", "p", "p", "q")

    def rs_copy(c, half, phase, k):
        s = axis_rs(half, phase)
        me = s["me"]
        if k < 4:
            j = (up(me, 2), up(me, 2), up(me), up(me, 3))[k]
            src = unit("g", c, half, phase, j, RS_PART[k])
        else:
            src = buf(c, half, phase, "tr" if k == 4 else "tl")
        return rc(src, buf(c, half, phase, RS_DST[k]), c, M_RS + half * 12 + phase * 6 + k,
                  s["r"] if k % 2 == 0 else s["l"])

    def rs_start(c, half, phase):
        for k in range(4):
            rs_copy(c, half, phase, k).start()

    def rs_mid(c, half, phase):
        me = axis_rs(half, phase)["me"]
        for k, j, part, arrived, out in ((0, up(me), "p", "al", "tr"), (1, up(me, 3), "q", "ar", "tl")):
            rs_copy(c, half, phase, k).wait_recv()
            total = unit("f", c, half, phase, j, part)[...] + buf(c, half, phase, arrived)[...].astype(F32)
            buf(c, half, phase, out)[...] = total.astype(BF16)
            rs_copy(c, half, phase, 4 + k).start()

    def rs_end(c, half, phase):
        me = axis_rs(half, phase)["me"]
        for k in range(2, 6):
            rs_copy(c, half, phase, k).wait_recv()
        for part, one, two in (("p", "cl", "br"), ("q", "bl", "cr")):
            total = (unit("f", c, half, phase, me, part)[...]
                     + buf(c, half, phase, one)[...].astype(F32) + buf(c, half, phase, two)[...].astype(F32))
            if phase == 0:
                at = pl.ds(0 if part == "p" else 2, 2)
                total = total.reshape(2, ROWS, 128)
                b["h"][c, half, at] = total
                b["hb"][c, half, at] = total.astype(BF16)
            else:
                at = pl.ds(0, 80) if part == "p" else pl.ds(80, 64)
                b["e"][c, at, pl.ds(half * 128, 128)] = total

    def z_copy(c):
        return rc(b["zs"].at[c], b["zr"].at[c], c, M_Z, dev(zz=1 - zh))

    def z_send(c):
        v = b["e"][c]
        b["zs"][c] = jnp.where(zh == 0, v[64:], v[:80]).astype(BF16)
        z_copy(c).start()

    def fix_copy(c, slot):
        return rc(b["fs"].at[c], b["gx"].at[c, slot], c, M_FIX, dev(cc=other))

    def gossip_copy(c, distance, rel, slot):
        to = core if rel == 0 else other
        return rc(b["gb"].at[c, to], b["gp"].at[distance - 1, c, slot], c,
                  M_GOS + (distance - 1) * 2 + rel, dev(r=up(rep, distance), cc=to))

    def z_done(c):
        z_copy(c).wait_recv()
        v = b["e"][c]
        r = b["zr"][c].astype(F32)
        total = jnp.where(zh == 0, v[:72], v[72:]) + jnp.where(zh == 0, r[:72], r[8:])
        first, last = total[:40], total[32:]
        b["gx"][c, core] = jnp.where(core == 0, first, last)
        b["fs"][c] = jnp.where(core == 0, last, first)
        b["gb"][c, 0] = total[:48].astype(BF16)
        b["gb"][c, 1] = total[24:].astype(BF16)
        for distance in (1, 2):
            for rel in (0, 1):
                gossip_copy(c, distance, rel, core).start()
        fix_copy(c, core).start()

    t = step_ref[0]
    learn_now = LEARN_RATE * (t.astype(F32) + 1.0) / WARM_SPAN
    near = lax.rem(t, 2) == 0

    def finish(c):
        fix_copy(c, other).wait_recv()
        for distance in (1, 2):
            for rel in (0, 1):
                gossip_copy(c, distance, rel, core if rel == 0 else other).wait_recv()
        for d in range(2):
            own = b["gx"][c, d]
            own = jnp.where(core == 0, own[:OWN], own[4:])
            peer = jnp.where(near, b["gp"][0, c, d], b["gp"][1, c, d]).astype(F32)
            peer = jnp.where(core == 0, peer[:OWN], peer[12:])
            for kv in range(2):
                cols = pl.ds(m16(kv * 1024 + d * 512 + c * 128, 128), 128)
                lanes = slice(kv * 128, kv * 128 + 128)
                peer_p = jnp.where(near, b["peer"][0, 0, :, cols], b["peer"][1, 0, :, cols])
                peer_m = jnp.where(near, b["peer"][0, 1, :, cols], b["peer"][1, 1, :, cols])
                mom = MOMENTUM_DECAY * b["m"][:, cols] + own[:, lanes]
                mom2 = MOMENTUM_DECAY * peer_m + peer[:, lanes]
                outm_ref[:, cols] = mom + mom2
                outp_ref[:, cols] = (b["p"][:, cols] - learn_now * mom) + (peer_p - learn_now * mom2)

    def exchange(k, slot):
        src = (tok_h.at[0], q_h.at[0, :, other_cols], cot_h.at[0, :, other_cols])[k]
        dst = b[("tok", "q", "cot")[k]].at[pl.ds(m16(slot * TOK, TOK), TOK), :]
        return pltpu.make_async_remote_copy(
            src_ref=src, dst_ref=dst, send_sem=gssem.at[k], recv_sem=grsem.at[k],
            device_id=dev(cc=other), device_id_type=MESH)

    def peer_copy(distance, k):
        at = 3 + (distance - 1) * 2 + k
        return pltpu.make_async_remote_copy(
            src_ref=(p_h, m_h)[k].at[0], dst_ref=b["peer"].at[distance - 1, k], send_sem=gssem.at[at],
            recv_sem=grsem.at[at], device_id=dev(r=up(rep, distance)), device_id_type=MESH)

    def each(*steps):
        def body(c, _):
            for step in steps:
                step(c)
            return 0

        lax.fori_loop(0, CH, body, 0)

    def halves(step, phase):
        def run(c):
            step(c, 0, phase)
            step(c, 1, phase)

        return run

    each(quad_send)
    for k in range(3):
        exchange(k, core).start()
    each(quad_done, halves(ag_start, 0))
    for distance in (1, 2):
        for k in range(2):
            peer_copy(distance, k).start()
    loads[2].wait()
    transpose_rows(core * 2)
    each(halves(ag_mid, 0))
    transpose_rows(core * 2 + 1)
    each(halves(ag_end, 0), halves(ag_start, 1))
    exchange(0, other).wait_recv()
    transpose_rows(other * 2)
    transpose_rows(other * 2 + 1)
    each(halves(ag_mid, 1))
    for k in (1, 2):
        exchange(k, other).wait_recv()
    for k in (1, 3, 4):
        loads[k].wait()

    def work(c):
        halves(ag_end, 1)(c)
        lax.fori_loop(0, 4, lambda s, _: (attend(c, s), 0)[1], 0)
        lax.fori_loop(0, 4, lambda yy, _: (gradient(c, yy), 0)[1], 0)
        halves(rs_start, 0)(c)

        @pl.when(c > 0)
        def _():
            halves(rs_mid, 0)(c - 1)

    each(work)
    halves(rs_mid, 0)(CH - 1)
    each(halves(rs_end, 0), halves(rs_start, 1))
    each(halves(rs_mid, 1))
    each(halves(rs_end, 1), z_send)
    each(z_done)
    for distance in (1, 2):
        for k in range(2):
            peer_copy(distance, k).wait_recv()
    each(finish)

    def drain(c):
        for k, (where, _, d) in enumerate(quad):
            rc(b["piece"].at[c, d], b["pin"].at[c, my_slot], c, M_QUAD + k, where).wait_send()
        for half in range(2):
            for phase in range(2):
                for k in range(4):
                    ag_copy(c, half, phase, k, up(axis_of(half, phase)["me"], (0, 0, 3, 1)[k])).wait_send()
                for k in range(6):
                    rs_copy(c, half, phase, k).wait_send()
        z_copy(c).wait_send()
        fix_copy(c, core).wait_send()
        for distance in (1, 2):
            for rel in (0, 1):
                gossip_copy(c, distance, rel, core).wait_send()

    each(drain)
    for k in range(3):
        exchange(k, core).wait_send()
    for distance in (1, 2):
        for k in range(2):
            peer_copy(distance, k).wait_send()


def shards(step_index, tokens, queries, cotangent, params, momentum):
    cos, sin = rope_tables()
    anywhere = pl.BlockSpec(memory_space=pl.ANY)
    vmem = pl.BlockSpec(memory_space=pltpu.VMEM)
    sum_p, sum_m = pl.pallas_call(
        kernel,
        out_shape=[jax.ShapeDtypeStruct((OWN, WIDE), F32)] * 2,
        in_specs=[pl.BlockSpec(memory_space=pltpu.SMEM)] + [anywhere] * 5 + [vmem] * 2,
        out_specs=[vmem, vmem],
        scratch_shapes=[pltpu.VMEM(shape, dtype) for shape, dtype in SCRATCH.values()]
        + [
            pltpu.SemaphoreType.DMA((CH, M_ALL)),
            pltpu.SemaphoreType.DMA((CH, M_ALL)),
            pltpu.SemaphoreType.DMA((7,)),
            pltpu.SemaphoreType.DMA((7,)),
            pltpu.SemaphoreType.DMA((5,)),
        ],
        compiler_params=pltpu.CompilerParams(
            collective_id=0, has_side_effects=True, vmem_limit_bytes=60 * 2**20),
        cost_estimate=pl.CostEstimate(flops=13 * 10**9, bytes_accessed=10**7, transcendentals=4 * 10**6),
    )(step_index, tokens, queries, cotangent, params, momentum, jnp.asarray(cos), jnp.asarray(sin))
    return 0.5 * sum_p[None], 0.5 * sum_m[None]


def solution(mesh):
    rows = P("rep", "fsdp", None)
    return jax.shard_map(
        shards,
        mesh=mesh,
        in_specs=(P(), rows, rows, rows, rows, rows),
        out_specs=(rows, rows),
        check_vma=False,
    )
```

time: 1300 us -> 127 us (0.10)
  waiting for transfers between devices: 1170 us -> 0 us
  Pallas kernels: 0 us -> 119 us
  matrix products: 48.6 us -> 0 us
  local copies, waits for them, and re-layouts: 48.6 us -> 5.6 us
  between operations: 15.6 us -> 1.29 us
    unnamed x3 -> x0, waiting for transfers between devices: 1030 us -> none
    pallas_call x0 -> x1, Pallas kernels: none -> 119 us  [shards(): pl.pallas_call(kernel, out_shape=[jax.ShapeDtypeStruct((OWN, WIDE), F32)]...]
    all_gather x1 -> x0, waiting for transfers between devices: 115 us -> none  [shards(): lax.all_gather(weight_shard, 'fsdp', axis=0, tiled=True)]
    dot_general x6 -> x0, matrix products: 48.6 us -> none  [the longest x1 18.8 us: shards(): jnp.einsum('bngqk,bqngd->bknd', score_low, query_low, preferred_element_t...]
    ppermute x1 -> x0, waiting for transfers between devices: 23.5 us -> none  [from_behind(): return lax.ppermute(block, axis, route)]
    unnamed x22 -> x4, local copies, waits for them, and re-layouts: 25.9 us -> 5.6 us
    another operation x5 -> x0, local copies, waits for them, and re-layouts: 15.6 us -> none  [the longest x2 10.6 us: shards(): query_low = queries[0].reshape(sequences, LENGTH, KVH, groups, HEAD)]
  transfers between devices with their start and end apart: 3 -> 0, of which waited for: 3 -> 0; matrix products, arithmetic and copies ran while one was open for 1% -> 0% of each run, Pallas kernels for 0% -> 0%
where the time goes in v1:
time: 127 us
  Pallas kernels  119 us (94%)
  local copies, waits for them, and re-layouts  5.6 us (4%)
  between operations  1.29 us (1%)
    pallas_call x1, Pallas kernels, shards(): pl.pallas_call(kernel, out_shape=[jax.ShapeDtypeStruct((OWN, WIDE), F32)]...  119 us
    unnamed x4, local copies, waits for them, and re-layouts  5.6 us

profile of v1, /device:TPU:1, one launch (start us, length us, event | category | flops | bytes accessed | tf_op | source)
XLA Modules:
  0.0 127.0 jit_solution(1145078038560330965)
XLA Ops:
  1.3 1.8 %copy.10.p_h = f32[1,36,2048]{2,1,0:T(8,128)} copy(f32[1,36,2048]{2,0,1:T(1,128)} %param.12) | data formatting | bytes 589824 | tf_op args[4]
  3.0 1.8 %copy.11.m_h = f32[1,36,2048]{2,1,0:T(8,128)} copy(f32[1,36,2048]{2,0,1:T(1,128)} %param.13) | data formatting | bytes 589824 | tf_op args[5]
  4.8 119.0 %shard_map.95 = (f32[36,2048]{1,0:T(8,128)}, f32[36,2048]{1,0:T(8,128)}) custom-call(s32[1]{0:T(128)S(6)} %copy.14.step_ref, bf16[1,512,2304]{2,1,0:T(8,128)(2,1)} %tok_h.1, bf16[1,512,2048]{2,1,0:T(8,128)(2,1)} %q_h.1, bf16[1,512,2048]{2,1,0:T(8,128)(2,1)} %cot_h.1, f32[1,36,2048]{2,1,0:T(8,128)} %copy.10.p_h, f32[1,36,2048]{2,1,0:T(8,128)} %copy.11.m_h, ...), custom_call_target="tpu_custom_call" | custom-call | flops 12999999488 | bytes 10000000 | tf_op jit(solution)/shard_map/pallas_call | solution.py:457
  123.9 1.1 multiply_bitcast_fusion
  125.0 1.0 copy.13
  126.0 1.0 copy.12

commit v2 on v1

--- a/solution.py
+++ b/solution.py
@@ -27,6 +27,8 @@
 ROWS = 144
 OWN = 36
 WIDE = 2048
+BLOCKS = WIDE // 128
+LINES = OWN * BLOCKS
 
 M_QUAD = 0
 M_AG = 3
@@ -56,11 +58,11 @@
     tok_t=((D, 2 * TOK), BF16),
     q=((2 * TOK, 1024), BF16),
     cot=((2 * TOK, 1024), BF16),
-    p=((OWN, WIDE), F32),
-    m=((OWN, WIDE), F32),
-    peer=((2, 2, OWN, WIDE), F32),
-    piece=((CH, 2, 48, 256), BF16),
-    pin=((CH, 4, 48, 256), BF16),
+    p=((LINES, 128), F32),
+    m=((LINES, 128), F32),
+    peer=((2, 2, LINES, 128), F32),
+    piece=((CH, 2, 80, 128), BF16),
+    pin=((CH, 4, 80, 128), BF16),
     w=((CH, 4, 576, 256), BF16),
     grads=((2 * TOK, 256), BF16),
     f=((CH, 4, 576, 256), F32),
@@ -70,10 +72,10 @@
     e=((CH, ROWS, 256), F32),
     zs=((CH, 80, 256), BF16),
     zr=((CH, 80, 256), BF16),
-    fs=((CH, 40, 256), F32),
-    gx=((CH, 2, 40, 256), F32),
-    gb=((CH, 2, 48, 256), BF16),
-    gp=((2, CH, 2, 48, 256), BF16),
+    fs=((CH, 72, 128), F32),
+    gx=((CH, 2, 72, 128), F32),
+    gb=((CH, 2, 80, 128), BF16),
+    gp=((2, CH, 2, 80, 128), BF16),
 )
 PARTS = ("al", "bl", "cl", "ar", "br", "cr", "tr", "tl")
 P_PARTS = ("al", "cl", "br", "tr")
@@ -118,12 +120,15 @@
             src_ref=src, dst_ref=dst, send_sem=ssem.at[c, k], recv_sem=rsem.at[c, k],
             device_id=where, device_id_type=MESH)
 
+    def strip(block):
+        return pl.ds(block, OWN, stride=BLOCKS)
+
     my_rows = pl.ds(m16(core * TOK, TOK), TOK)
     my_cols = pl.ds(m16(core * 1024, 1024), 1024)
     other_cols = pl.ds(m16(other * 1024, 1024), 1024)
     loads = [
-        pltpu.make_async_copy(p_h.at[0], b["p"], lsem.at[0]),
-        pltpu.make_async_copy(m_h.at[0], b["m"], lsem.at[1]),
+        pltpu.make_async_copy(p_h, b["p"], lsem.at[0]),
+        pltpu.make_async_copy(m_h, b["m"], lsem.at[1]),
         pltpu.make_async_copy(tok_h.at[0], b["tok"].at[my_rows, :], lsem.at[2]),
         pltpu.make_async_copy(q_h.at[0, :, my_cols], b["q"].at[my_rows, :], lsem.at[3]),
         pltpu.make_async_copy(cot_h.at[0, :, my_cols], b["cot"].at[my_rows, :], lsem.at[4]),
@@ -141,10 +146,9 @@
     loads[0].wait()
     for c in range(CH):
         for d in range(2):
-            k0 = d * 512 + c * 128
-            v = jnp.concatenate([b["p"][:, k0:k0 + 128], b["p"][:, 1024 + k0:1024 + k0 + 128]], axis=1)
-            v = jnp.concatenate([v, jnp.zeros((12, 256), F32)], axis=0)
-            b["piece"][c, d] = v.astype(BF16)
+            at = d * 4 + c
+            v = [b["p"][strip(at), :], b["p"][strip(8 + at), :], jnp.zeros((8, 128), F32)]
+            b["piece"][c, d] = jnp.concatenate(v, axis=0).astype(BF16)
 
     pl.semaphore_wait(barrier, len(partners))
 
@@ -161,8 +165,10 @@
         for k, (where, slot, d) in enumerate(quad):
             rc(b["piece"].at[c, d], b["pin"].at[c, slot], c, M_QUAD + k, where).wait_recv()
         b["pin"][c, my_slot] = b["piece"][c, core]
-        v = [b["pin"][c, s].astype(F32)[:OWN] for s in range(4)]
-        b["w"][c, y, pl.ds(m16(x * ROWS), ROWS), :] = jnp.concatenate(v, axis=0).astype(BF16)
+        v = [b["pin"][c, s].astype(F32) for s in range(4)]
+        for kv in range(2):
+            block = jnp.concatenate([u[kv * OWN:(kv + 1) * OWN] for u in v], axis=0)
+            b["w"][c, y, pl.ds(m16(x * ROWS), ROWS), pl.ds(kv * 128, 128)] = block.astype(BF16)
 
     def w_unit(c, half, phase, j, part):
         lanes = pl.ds(half * 128, 128)
@@ -323,11 +329,12 @@
         v = b["e"][c]
         r = b["zr"][c].astype(F32)
         total = jnp.where(zh == 0, v[:72], v[72:]) + jnp.where(zh == 0, r[:72], r[8:])
-        first, last = total[:40], total[32:]
+        first, last = (jnp.concatenate([total[r:r + OWN, :128], total[r:r + OWN, 128:]], axis=0) for r in (0, OWN))
+        pad = jnp.zeros((8, 128), F32)
+        b["gb"][c, 0] = jnp.concatenate([first, pad], axis=0).astype(BF16)
+        b["gb"][c, 1] = jnp.concatenate([last, pad], axis=0).astype(BF16)
+        b["fs"][c] = jnp.where(core == 0, last, first)
         b["gx"][c, core] = jnp.where(core == 0, first, last)
-        b["fs"][c] = jnp.where(core == 0, last, first)
-        b["gb"][c, 0] = total[:48].astype(BF16)
-        b["gb"][c, 1] = total[24:].astype(BF16)
         for distance in (1, 2):
             for rel in (0, 1):
                 gossip_copy(c, distance, rel, core).start()
@@ -344,18 +351,15 @@
                 gossip_copy(c, distance, rel, core if rel == 0 else other).wait_recv()
         for d in range(2):
             own = b["gx"][c, d]
-            own = jnp.where(core == 0, own[:OWN], own[4:])
             peer = jnp.where(near, b["gp"][0, c, d], b["gp"][1, c, d]).astype(F32)
-            peer = jnp.where(core == 0, peer[:OWN], peer[12:])
             for kv in range(2):
-                cols = pl.ds(m16(kv * 1024 + d * 512 + c * 128, 128), 128)
-                lanes = slice(kv * 128, kv * 128 + 128)
-                peer_p = jnp.where(near, b["peer"][0, 0, :, cols], b["peer"][1, 0, :, cols])
-                peer_m = jnp.where(near, b["peer"][0, 1, :, cols], b["peer"][1, 1, :, cols])
-                mom = MOMENTUM_DECAY * b["m"][:, cols] + own[:, lanes]
-                mom2 = MOMENTUM_DECAY * peer_m + peer[:, lanes]
-                outm_ref[:, cols] = mom + mom2
-                outp_ref[:, cols] = (b["p"][:, cols] - learn_now * mom) + (peer_p - learn_now * mom2)
+                at = strip(kv * 8 + d * 4 + c)
+                peer_p = jnp.where(near, b["peer"][0, 0, at, :], b["peer"][1, 0, at, :])
+                peer_m = jnp.where(near, b["peer"][0, 1, at, :], b["peer"][1, 1, at, :])
+                mom = MOMENTUM_DECAY * b["m"][at, :] + own[kv * OWN:(kv + 1) * OWN]
+                mom2 = MOMENTUM_DECAY * peer_m + peer[kv * OWN:(kv + 1) * OWN]
+                outm_ref[at, :] = mom + mom2
+                outp_ref[at, :] = (b["p"][at, :] - learn_now * mom) + (peer_p - learn_now * mom2)
 
     def exchange(k, slot):
         src = (tok_h.at[0], q_h.at[0, :, other_cols], cot_h.at[0, :, other_cols])[k]
@@ -367,7 +371,7 @@
     def peer_copy(distance, k):
         at = 3 + (distance - 1) * 2 + k
         return pltpu.make_async_remote_copy(
-            src_ref=(p_h, m_h)[k].at[0], dst_ref=b["peer"].at[distance - 1, k], send_sem=gssem.at[at],
+            src_ref=(p_h, m_h)[k], dst_ref=b["peer"].at[distance - 1, k], send_sem=gssem.at[at],
             recv_sem=grsem.at[at], device_id=dev(r=up(rep, distance)), device_id_type=MESH)
 
     def each(*steps):
@@ -385,47 +389,87 @@
 
         return run
 
+    def when(condition, *steps):
+        def run():
+            for step, c in steps:
+                step(c)
+
+        pl.when(condition)(run)
+
+    ag0s, ag0m, ag0e = (halves(step, 0) for step in (ag_start, ag_mid, ag_end))
+    ag1s, ag1m, ag1e = (halves(step, 1) for step in (ag_start, ag_mid, ag_end))
+    rs0s, rs0m, rs0e = (halves(step, 0) for step in (rs_start, rs_mid, rs_end))
+    rs1s, rs1m, rs1e = (halves(step, 1) for step in (rs_start, rs_mid, rs_end))
+
     each(quad_send)
     for k in range(3):
         exchange(k, core).start()
-    each(quad_done, halves(ag_start, 0))
+    for c in range(2):
+        quad_done(c)
+        ag0s(c)
+    loads[2].wait()
+    ag0m(0)
+    quad_done(2)
+    ag0s(2)
+    ag0e(0)
+    ag1s(0)
+    ag0m(1)
+    transpose_rows(core * 2)
+    quad_done(3)
+    ag0s(3)
+    ag0e(1)
+    ag1s(1)
     for distance in (1, 2):
         for k in range(2):
             peer_copy(distance, k).start()
-    loads[2].wait()
-    transpose_rows(core * 2)
-    each(halves(ag_mid, 0))
     transpose_rows(core * 2 + 1)
-    each(halves(ag_end, 0), halves(ag_start, 1))
+    ag1m(0)
     exchange(0, other).wait_recv()
     transpose_rows(other * 2)
+    ag0m(2)
     transpose_rows(other * 2 + 1)
-    each(halves(ag_mid, 1))
+    ag0m(3)
     for k in (1, 2):
         exchange(k, other).wait_recv()
     for k in (1, 3, 4):
         loads[k].wait()
 
     def work(c):
-        halves(ag_end, 1)(c)
-        lax.fori_loop(0, 4, lambda s, _: (attend(c, s), 0)[1], 0)
-        lax.fori_loop(0, 4, lambda yy, _: (gradient(c, yy), 0)[1], 0)
-        halves(rs_start, 0)(c)
-
-        @pl.when(c > 0)
-        def _():
-            halves(rs_mid, 0)(c - 1)
+        ag1e(c)
+        attend(c, 0)
+        when(c + 1 < CH, (ag1m, c + 1))
+        attend(c, 1)
+        when(c > 0, (rs0m, c - 1))
+        when(c + 2 < CH, (ag0e, c + 2), (ag1s, c + 2))
+        attend(c, 2)
+        when(c > 1, (z_done, c - 2))
+        attend(c, 3)
+        when(c > 0, (rs0e, c - 1), (rs1s, c - 1))
+        gradient(c, 0)
+        gradient(c, 1)
+        when(c > 0, (rs1m, c - 1))
+        gradient(c, 2)
+        gradient(c, 3)
+        rs0s(c)
+        when(c > 0, (rs1e, c - 1), (z_send, c - 1))
 
     each(work)
-    halves(rs_mid, 0)(CH - 1)
-    each(halves(rs_end, 0), halves(rs_start, 1))
-    each(halves(rs_mid, 1))
-    each(halves(rs_end, 1), z_send)
-    each(z_done)
+    last = CH - 1
+    rs0m(last)
+    z_done(last - 1)
+    rs0e(last)
+    rs1s(last)
     for distance in (1, 2):
         for k in range(2):
             peer_copy(distance, k).wait_recv()
-    each(finish)
+    for c in range(last - 1):
+        finish(c)
+    rs1m(last)
+    finish(last - 1)
+    rs1e(last)
+    z_send(last)
+    z_done(last)
+    finish(last)
 
     def drain(c):
         for k, (where, _, d) in enumerate(quad):
@@ -456,7 +500,7 @@
     vmem = pl.BlockSpec(memory_space=pltpu.VMEM)
     sum_p, sum_m = pl.pallas_call(
         kernel,
-        out_shape=[jax.ShapeDtypeStruct((OWN, WIDE), F32)] * 2,
+        out_shape=[jax.ShapeDtypeStruct((LINES, 128), F32)] * 2,
         in_specs=[pl.BlockSpec(memory_space=pltpu.SMEM)] + [anywhere] * 5 + [vmem] * 2,
         out_specs=[vmem, vmem],
         scratch_shapes=[pltpu.VMEM(shape, dtype) for shape, dtype in SCRATCH.values()]
@@ -470,8 +514,9 @@
         compiler_params=pltpu.CompilerParams(
             collective_id=0, has_side_effects=True, vmem_limit_bytes=60 * 2**20),
         cost_estimate=pl.CostEstimate(flops=13 * 10**9, bytes_accessed=10**7, transcendentals=4 * 10**6),
-    )(step_index, tokens, queries, cotangent, params, momentum, jnp.asarray(cos), jnp.asarray(sin))
-    return 0.5 * sum_p[None], 0.5 * sum_m[None]
+    )(step_index, tokens, queries, cotangent, params.reshape(LINES, 128), momentum.reshape(LINES, 128),
+      jnp.asarray(cos), jnp.asarray(sin))
+    return (0.5 * sum_p).reshape(1, OWN, WIDE), (0.5 * sum_m).reshape(1, OWN, WIDE)
 
 
 def solution(mesh):

time: 127 us -> 124 us (0.976)
  local copies, waits for them, and re-layouts: 5.6 us -> 0 us
  Pallas kernels: 119 us -> 121 us
    unnamed x4 -> x0, local copies, waits for them, and re-layouts: 5.6 us -> none
    pallas_call x1, Pallas kernels: 119 us -> 121 us  [shards(): pl.pallas_call(kernel, out_shape=[jax.ShapeDtypeStruct((LINES, 128), F32)...]
where the time goes in v2:
time: 124 us
  Pallas kernels  121 us (98%)
  other arithmetic  1.9 us (2%)
  between operations  1.28 us (1%)
    pallas_call x1, Pallas kernels, shards(): pl.pallas_call(kernel, out_shape=[jax.ShapeDtypeStruct((LINES, 128), F32)...  121 us

profile of v2, /device:TPU:1, one launch (start us, length us, event | category | flops | bytes accessed | tf_op | source)
XLA Modules:
  0.0 124.1 jit_solution(3022867980978329098)
XLA Ops:
  1.3 121.0 %shard_map.95 = (f32[576,128]{1,0:T(8,128)}, f32[576,128]{1,0:T(8,128)}) custom-call(s32[1]{0:T(128)S(6)} %copy.14.step_ref, bf16[1,512,2304]{2,1,0:T(8,128)(2,1)} %tok_h.1, bf16[1,512,2048]{2,1,0:T(8,128)(2,1)} %q_h.1, bf16[1,512,2048]{2,1,0:T(8,128)(2,1)} %cot_h.1, f32[576,128]{1,0:T(8,128)} %bitcast.6, f32[576,128]{1,0:T(8,128)} %bitcast.7, ...), custom_call_target="tpu_custom_call" | custom-call | flops 12999999488 | bytes 10000000 | tf_op jit(solution)/shard_map/pallas_call | solution.py:501
  122.2 1.9 %broadcast_multiply_fusion = (f32[576,128]{1,0:T(8,128)}, f32[576,128]{1,0:T(8,128)}) fusion(f32[576,128]{1,0:T(8,128)} %get-tuple-element.5, f32[576,128]{1,0:T(8,128)} %get-tuple-element.4), kind=kLoop, calls=%fused_computation | loop fusion | flops 147456 | bytes 1179648 | tf_op jit(solution)/shard_map/mul | solution.py:519

commit v3 on v2

--- a/solution.py
+++ b/solution.py
@@ -20,6 +20,7 @@
 LEARN_RATE = 0.1
 WARM_SPAN = 64.0
 MOMENTUM_DECAY = 0.9
+LOG2E = 1.4426950408889634
 
 D = 2304
 TOK = 512
@@ -28,7 +29,6 @@
 OWN = 36
 WIDE = 2048
 BLOCKS = WIDE // 128
-LINES = OWN * BLOCKS
 
 M_QUAD = 0
 M_AG = 3
@@ -36,7 +36,7 @@
 M_Z = 43
 M_FIX = 44
 M_GOS = 45
-M_ALL = 49
+M_ALL = 47
 
 
 def rope_tables():
@@ -58,12 +58,17 @@
     tok_t=((D, 2 * TOK), BF16),
     q=((2 * TOK, 1024), BF16),
     cot=((2 * TOK, 1024), BF16),
-    p=((LINES, 128), F32),
-    m=((LINES, 128), F32),
-    peer=((2, 2, LINES, 128), F32),
+    p=((BLOCKS, OWN, 128), F32),
+    m=((BLOCKS, OWN, 128), F32),
+    peer=((2, BLOCKS, OWN, 128), F32),
+    out_p=((BLOCKS, OWN, 128), F32),
+    out_m=((BLOCKS, OWN, 128), F32),
+    cos=((LENGTH, HEAD), F32),
+    sin=((LENGTH, HEAD), F32),
     piece=((CH, 2, 80, 128), BF16),
     pin=((CH, 4, 80, 128), BF16),
     w=((CH, 4, 576, 256), BF16),
+    joined=((2 * TOK, 256), BF16),
     grads=((2 * TOK, 256), BF16),
     f=((CH, 4, 576, 256), F32),
     g=((CH, 4, 576, 256), BF16),
@@ -75,7 +80,7 @@
     fs=((CH, 72, 128), F32),
     gx=((CH, 2, 72, 128), F32),
     gb=((CH, 2, 80, 128), BF16),
-    gp=((2, CH, 2, 80, 128), BF16),
+    gp=((CH, 2, 80, 128), BF16),
 )
 PARTS = ("al", "bl", "cl", "ar", "br", "cr", "tr", "tl")
 P_PARTS = ("al", "cl", "br", "tr")
@@ -87,9 +92,9 @@
 NAMES = tuple(SCRATCH)
 
 
-def kernel(step_ref, tok_h, q_h, cot_h, p_h, m_h, cos_ref, sin_ref, outp_ref, outm_ref, *scratch):
+def kernel(distance, step_ref, tok_h, q_h, cot_h, p_h, m_h, cos_h, sin_h, outp_h, outm_h, *scratch):
     b = dict(zip(NAMES, scratch))
-    ssem, rsem, gssem, grsem, lsem = scratch[len(NAMES):]
+    ssem, rsem, gssem, grsem, lsem, psem, osem = scratch[len(NAMES):]
     rep = lax.axis_index("rep")
     f = lax.axis_index("fsdp")
     core = lax.rem(f, 2)
@@ -120,37 +125,42 @@
             src_ref=src, dst_ref=dst, send_sem=ssem.at[c, k], recv_sem=rsem.at[c, k],
             device_id=where, device_id_type=MESH)
 
-    def strip(block):
-        return pl.ds(block, OWN, stride=BLOCKS)
-
     my_rows = pl.ds(m16(core * TOK, TOK), TOK)
     my_cols = pl.ds(m16(core * 1024, 1024), 1024)
     other_cols = pl.ds(m16(other * 1024, 1024), 1024)
     loads = [
-        pltpu.make_async_copy(p_h, b["p"], lsem.at[0]),
-        pltpu.make_async_copy(m_h, b["m"], lsem.at[1]),
         pltpu.make_async_copy(tok_h.at[0], b["tok"].at[my_rows, :], lsem.at[2]),
         pltpu.make_async_copy(q_h.at[0, :, my_cols], b["q"].at[my_rows, :], lsem.at[3]),
         pltpu.make_async_copy(cot_h.at[0, :, my_cols], b["cot"].at[my_rows, :], lsem.at[4]),
     ]
+    loads += [
+        pltpu.make_async_copy(cos_h, b["cos"], lsem.at[0]),
+        pltpu.make_async_copy(sin_h, b["sin"], lsem.at[1]),
+    ]
+    strips = [[pltpu.make_async_copy(ref.at[:, k, :], b["pm"[i]].at[k], psem.at[i, k]) for k in range(BLOCKS)]
+              for i, ref in enumerate((p_h, m_h))]
+    order = [kd + c for c in range(CH) for kd in (0, 4, 8, 12)]
+    for k in order:
+        strips[0][k].start()
     for load in loads:
         load.start()
+    for k in order:
+        strips[1][k].start()
 
     barrier = pltpu.get_barrier_semaphore()
     partners = [dev(cc=other), dev(zz=1 - zh), dev(zz=1 - zh, cc=other)]
     partners += [side[a][d] for a in ("x", "y") for d in ("r", "l")]
-    partners += [dev(r=up(rep, d), cc=cc) for d in (1, 2, 3) for cc in (core, other)]
+    partners += [dev(xx=up(x, 2)), dev(yy=up(y, 2))]
+    partners += [dev(r=up(rep, d), cc=cc) for d in sorted({distance, 4 - distance}) for cc in (core, other)]
     for partner in partners:
         pl.semaphore_signal(barrier, inc=1, device_id=partner, device_id_type=MESH)
 
-    loads[0].wait()
-    for c in range(CH):
+    def make_pieces(c):
+        for kd in (0, 4, 8, 12):
+            strips[0][kd + c].wait()
         for d in range(2):
-            at = d * 4 + c
-            v = [b["p"][strip(at), :], b["p"][strip(8 + at), :], jnp.zeros((8, 128), F32)]
+            v = [b["p"][d * 4 + c], b["p"][8 + d * 4 + c], jnp.zeros((8, 128), F32)]
             b["piece"][c, d] = jnp.concatenate(v, axis=0).astype(BF16)
-
-    pl.semaphore_wait(barrier, len(partners))
 
     quad = [(dev(cc=other), zh * 2 + other, other),
             (dev(zz=1 - zh), (1 - zh) * 2 + core, core),
@@ -184,6 +194,9 @@
         at, n = dict(all=(0, 4), p=(0, 2), q=(2, 2))[part]
         return w.at[c, pl.ds(at, n), pl.ds(m16(j * ROWS), ROWS), lanes]
 
+    def far(half, phase):
+        return dev(xx=up(x, 2)) if half == phase else dev(yy=up(y, 2))
+
     def ag_copy(c, half, phase, k, j):
         s = axis_of(half, phase)
         unit = w_unit(c, half, phase, j, ("all", "all", "p", "q")[k])
@@ -216,43 +229,52 @@
 
         lax.fori_loop(0, D // 256, one, 0)
 
-    causal = lax.broadcasted_iota(jnp.int32, (LENGTH, LENGTH), 0) <= lax.broadcasted_iota(
-        jnp.int32, (LENGTH, LENGTH), 1)
+    half_len = LENGTH // 2
+    triangle = lax.broadcasted_iota(jnp.int32, (half_len, LENGTH), 0) <= lax.rem(
+        lax.broadcasted_iota(jnp.int32, (half_len, LENGTH), 1), half_len)
     scale_in = D ** (-0.5)
 
     def nt(a, bb):
         return lax.dot_general(a, bb, (((1,), (1,)), ((), ())), preferred_element_type=F32)
 
+    def project(c):
+        w = b["w"][c].reshape(D, 256)
+        b["joined"][...] = (jnp.dot(b["tok"][...], w, preferred_element_type=F32) * scale_in).astype(BF16)
+
     def attend(c, s):
         rows = pl.ds(m16(s * 256, 256), 256)
-        w = b["w"][c].reshape(D, 256)
-        joined = (jnp.dot(b["tok"][rows, :], w, preferred_element_type=F32) * scale_in).astype(BF16)
+        joined = b["joined"][rows, :]
         key = joined[:, :HEAD].astype(F32)
         val = joined[:, HEAD:]
-        cos, sin = cos_ref[...], sin_ref[...]
+        cos, sin = b["cos"][...], b["sin"][...]
         rot = (key * cos + pltpu.roll(key, 64, 1) * sin).astype(BF16)
-        d_val = jnp.zeros((LENGTH, HEAD), F32)
-        d_rot = jnp.zeros((LENGTH, HEAD), F32)
-        for head in range(2):
-            cols = pl.ds(m16(c * 256 + head * 128, 128), 128)
-            qh = b["q"][rows, cols]
-            ch = b["cot"][rows, cols]
-            bent = jnp.tanh(nt(rot, qh) * (SCORE_SCALE / SOFT_CAP))
-            weights = jnp.where(causal, jnp.exp(SOFT_CAP * bent), 0.0)
+        d_val, d_rot = [], []
+        for block in range(2):
+            at = pl.ds(m16(s * LENGTH + block * half_len, half_len), half_len)
+            cols = [pl.ds(m16(c * 256 + head * 128, 128), 128) for head in range(2)]
+            qh = jnp.concatenate([b["q"][at, col] for col in cols], axis=0)
+            ch = jnp.concatenate([b["cot"][at, col] for col in cols], axis=0)
+            keys = half_len * (block + 1)
+            bent = jnp.tanh(nt(rot[:keys], qh) * (SCORE_SCALE / SOFT_CAP))
+            weights = jnp.exp2(bent * (SOFT_CAP * LOG2E))
+            masked = jnp.where(triangle, weights[keys - half_len:], 0.0)
+            weights = masked if block == 0 else jnp.concatenate([weights[:half_len], masked], axis=0)
             shares = weights * (1.0 / jnp.sum(weights, axis=0, keepdims=True))
-            d_val += jnp.dot(shares.astype(BF16), ch, preferred_element_type=F32)
-            share_grad = nt(val, ch)
+            d_val.append(jnp.dot(shares.astype(BF16), ch, preferred_element_type=F32))
+            share_grad = nt(val[:keys], ch)
             mean = jnp.sum(shares * share_grad, axis=0, keepdims=True)
-            score = shares * (share_grad - mean) * ((1.0 - bent * bent) * SCORE_SCALE)
-            d_rot += jnp.dot(score.astype(BF16), qh, preferred_element_type=F32)
+            score = shares * (share_grad - mean) * (SCORE_SCALE - bent * bent * SCORE_SCALE)
+            d_rot.append(jnp.dot(score.astype(BF16), qh, preferred_element_type=F32))
+        d_val, d_rot = (jnp.concatenate([hi[:half_len] + lo, hi[half_len:]], axis=0) for lo, hi in (d_val, d_rot))
         d_key = d_rot * cos - pltpu.roll(d_rot, 64, 1) * sin
         b["grads"][rows, :] = (jnp.concatenate([d_key, d_val], axis=1) * scale_in).astype(BF16)
 
-    def gradient(c, yy):
-        rows = pl.ds(m16(yy * 576, 64), 576)
-        v = jnp.dot(b["tok_t"][rows, :], b["grads"][...], preferred_element_type=F32)
-        b["f"][c, yy] = v
-        b["g"][c, yy] = v.astype(BF16)
+    def gradient(c, part):
+        rows = pl.ds(m16(part * 1152, 128), 1152)
+        v = jnp.dot(b["tok_t"][rows, :], b["grads"][...], preferred_element_type=F32).reshape(2, 576, 256)
+        at = pl.ds(part * 2, 2)
+        b["f"][c, at] = v
+        b["g"][c, at] = v.astype(BF16)
 
     def unit(name, c, half, phase, j, part):
         if phase == 0:
@@ -319,10 +341,10 @@
     def fix_copy(c, slot):
         return rc(b["fs"].at[c], b["gx"].at[c, slot], c, M_FIX, dev(cc=other))
 
-    def gossip_copy(c, distance, rel, slot):
+    def gossip_copy(c, rel, slot):
         to = core if rel == 0 else other
-        return rc(b["gb"].at[c, to], b["gp"].at[distance - 1, c, slot], c,
-                  M_GOS + (distance - 1) * 2 + rel, dev(r=up(rep, distance), cc=to))
+        return rc(b["gb"].at[c, to], b["gp"].at[c, slot], c, M_GOS + rel,
+                  dev(r=up(rep, distance), cc=to))
 
     def z_done(c):
         z_copy(c).wait_recv()
@@ -335,31 +357,31 @@
         b["gb"][c, 1] = jnp.concatenate([last, pad], axis=0).astype(BF16)
         b["fs"][c] = jnp.where(core == 0, last, first)
         b["gx"][c, core] = jnp.where(core == 0, first, last)
-        for distance in (1, 2):
-            for rel in (0, 1):
-                gossip_copy(c, distance, rel, core).start()
+        for rel in (0, 1):
+            gossip_copy(c, rel, core).start()
         fix_copy(c, core).start()
 
     t = step_ref[0]
     learn_now = LEARN_RATE * (t.astype(F32) + 1.0) / WARM_SPAN
-    near = lax.rem(t, 2) == 0
+
+    def out_copy(i, k):
+        return pltpu.make_async_copy(b[("out_p", "out_m")[i]].at[k], (outp_h, outm_h)[i].at[:, k, :], osem.at[i, k])
 
     def finish(c):
         fix_copy(c, other).wait_recv()
-        for distance in (1, 2):
-            for rel in (0, 1):
-                gossip_copy(c, distance, rel, core if rel == 0 else other).wait_recv()
+        for rel in (0, 1):
+            gossip_copy(c, rel, core if rel == 0 else other).wait_recv()
         for d in range(2):
             own = b["gx"][c, d]
-            peer = jnp.where(near, b["gp"][0, c, d], b["gp"][1, c, d]).astype(F32)
+            peer = b["gp"][c, d].astype(F32)
             for kv in range(2):
-                at = strip(kv * 8 + d * 4 + c)
-                peer_p = jnp.where(near, b["peer"][0, 0, at, :], b["peer"][1, 0, at, :])
-                peer_m = jnp.where(near, b["peer"][0, 1, at, :], b["peer"][1, 1, at, :])
-                mom = MOMENTUM_DECAY * b["m"][at, :] + own[kv * OWN:(kv + 1) * OWN]
-                mom2 = MOMENTUM_DECAY * peer_m + peer[kv * OWN:(kv + 1) * OWN]
-                outm_ref[at, :] = mom + mom2
-                outp_ref[at, :] = (b["p"][at, :] - learn_now * mom) + (peer_p - learn_now * mom2)
+                at = kv * 8 + d * 4 + c
+                mom = MOMENTUM_DECAY * b["m"][at] + own[kv * OWN:(kv + 1) * OWN]
+                mom2 = MOMENTUM_DECAY * b["peer"][1, at] + peer[kv * OWN:(kv + 1) * OWN]
+                b["out_m"][at] = mom + mom2
+                b["out_p"][at] = (b["p"][at] - learn_now * mom) + (b["peer"][0, at] - learn_now * mom2)
+                for i in range(2):
+                    out_copy(i, at).start()
 
     def exchange(k, slot):
         src = (tok_h.at[0], q_h.at[0, :, other_cols], cot_h.at[0, :, other_cols])[k]
@@ -368,10 +390,10 @@
             src_ref=src, dst_ref=dst, send_sem=gssem.at[k], recv_sem=grsem.at[k],
             device_id=dev(cc=other), device_id_type=MESH)
 
-    def peer_copy(distance, k):
-        at = 3 + (distance - 1) * 2 + k
+    def peer_copy(k):
+        at = 3 + k
         return pltpu.make_async_remote_copy(
-            src_ref=(p_h, m_h)[k], dst_ref=b["peer"].at[distance - 1, k], send_sem=gssem.at[at],
+            src_ref=b["pm"[k]], dst_ref=b["peer"].at[k], send_sem=gssem.at[at],
             recv_sem=grsem.at[at], device_id=dev(r=up(rep, distance)), device_id_type=MESH)
 
     def each(*steps):
@@ -389,6 +411,58 @@
 
         return run
 
+    def agd_copy(c, half, phase, k, j):
+        s = axis_of(half, phase)
+        block = w_unit(c, half, phase, j, "all")
+        return rc(block, block, c, M_AG + half * 8 + phase * 4 + k, (s["r"], s["l"], far(half, phase))[k])
+
+    def agd_start(c, half, phase):
+        me = axis_of(half, phase)["me"]
+        for k in (2, 0, 1):
+            agd_copy(c, half, phase, k, me).start()
+
+    def agd_end(c, half, phase):
+        me = axis_of(half, phase)["me"]
+        for k, by in ((0, 3), (1, 1), (2, 2)):
+            agd_copy(c, half, phase, k, up(me, by)).wait_recv()
+
+    def rsd_copy(c, half, phase, k, part):
+        s = axis_rs(half, phase)
+        me = s["me"]
+        j = (up(me), up(me, 3), up(me, 2))[k]
+        src = unit("g", c, half, phase, j, part)
+        name = {"p": ("al", "br", "cl"), "q": ("ar", "bl", "cr")}[part][k]
+        return rc(src, buf(c, half, phase, name), c, M_RS + half * 12 + phase * 6 + k * 2 + (part == "q"),
+                  (s["r"], s["l"], far(half, phase))[k])
+
+    def rsd_start(c, half, phase):
+        for k in (2, 0, 1):
+            for part in ("p", "q"):
+                rsd_copy(c, half, phase, k, part).start()
+
+    def rsd_end(c, half, phase):
+        me = axis_rs(half, phase)["me"]
+        for part in ("p", "q"):
+            for k in range(3):
+                rsd_copy(c, half, phase, k, part).wait_recv()
+        for part, names in (("p", ("al", "br", "cl")), ("q", ("ar", "bl", "cr"))):
+            total = unit("f", c, half, phase, me, part)[...]
+            for name in names:
+                total += buf(c, half, phase, name)[...].astype(F32)
+            if phase == 0:
+                at = pl.ds(0 if part == "p" else 2, 2)
+                total = total.reshape(2, ROWS, 128)
+                b["h"][c, half, at] = total
+                b["hb"][c, half, at] = total.astype(BF16)
+            else:
+                at = pl.ds(0, 80) if part == "p" else pl.ds(80, 64)
+                b["e"][c, at, pl.ds(half * 128, 128)] = total
+
+    agd0s, agd0e = (halves(step, 0) for step in (agd_start, agd_end))
+    ag1s, ag1m, ag1e = (halves(step, 1) for step in (ag_start, ag_mid, ag_end))
+    rs0s, rs0m, rs0e = (halves(step, 0) for step in (rs_start, rs_mid, rs_end))
+    rsd1s, rsd1e = (halves(step, 1) for step in (rsd_start, rsd_end))
+
     def when(condition, *steps):
         def run():
             for step, c in steps:
@@ -396,77 +470,85 @@
 
         pl.when(condition)(run)
 
-    ag0s, ag0m, ag0e = (halves(step, 0) for step in (ag_start, ag_mid, ag_end))
-    ag1s, ag1m, ag1e = (halves(step, 1) for step in (ag_start, ag_mid, ag_end))
-    rs0s, rs0m, rs0e = (halves(step, 0) for step in (rs_start, rs_mid, rs_end))
-    rs1s, rs1m, rs1e = (halves(step, 1) for step in (rs_start, rs_mid, rs_end))
-
-    each(quad_send)
-    for k in range(3):
+    make_pieces(0)
+    pl.semaphore_wait(barrier, len(partners))
+    quad_send(0)
+    for c in range(1, CH):
+        make_pieces(c)
+        quad_send(c)
+    exchange(0, core).start()
+    loads[0].wait()
+    quad_done(0)
+    agd0s(0)
+    transpose_rows(core * 2)
+    for k in (1, 2):
         exchange(k, core).start()
-    for c in range(2):
-        quad_done(c)
-        ag0s(c)
-    loads[2].wait()
-    ag0m(0)
+    quad_done(1)
+    agd0s(1)
+    agd0e(0)
+    ag1s(0)
     quad_done(2)
-    ag0s(2)
-    ag0e(0)
-    ag1s(0)
-    ag0m(1)
-    transpose_rows(core * 2)
+    agd0s(2)
+    transpose_rows(core * 2 + 1)
+    agd0e(1)
+    ag1s(1)
     quad_done(3)
-    ag0s(3)
-    ag0e(1)
-    ag1s(1)
-    for distance in (1, 2):
-        for k in range(2):
-            peer_copy(distance, k).start()
-    transpose_rows(core * 2 + 1)
+    agd0s(3)
     ag1m(0)
+    for k in range(BLOCKS):
+        strips[1][k].wait()
+    for k in range(2):
+        peer_copy(k).start()
     exchange(0, other).wait_recv()
     transpose_rows(other * 2)
-    ag0m(2)
+    agd0e(2)
+    ag1s(2)
     transpose_rows(other * 2 + 1)
-    ag0m(3)
     for k in (1, 2):
         exchange(k, other).wait_recv()
-    for k in (1, 3, 4):
+    for k in (1, 2, 3, 4):
         loads[k].wait()
 
     def work(c):
         ag1e(c)
-        attend(c, 0)
-        when(c + 1 < CH, (ag1m, c + 1))
-        attend(c, 1)
-        when(c > 0, (rs0m, c - 1))
-        when(c + 2 < CH, (ag0e, c + 2), (ag1s, c + 2))
-        attend(c, 2)
-        when(c > 1, (z_done, c - 2))
-        attend(c, 3)
-        when(c > 0, (rs0e, c - 1), (rs1s, c - 1))
-        gradient(c, 0)
-        gradient(c, 1)
-        when(c > 0, (rs1m, c - 1))
-        gradient(c, 2)
-        gradient(c, 3)
+
+        project(c)
+        when(c == 0, (ag1m, 1))
+        when(c > 1, (rsd1e, c - 2), (z_send, c - 2))
+
+        def pair(i, _):
+            attend(c, 2 * i)
+            attend(c, 2 * i + 1)
+            when((c == 0) & (i == 0), (agd0e, 3), (ag1s, 3))
+            when((c == 1) & (i == 0), (ag1m, 3))
+            when((c > 0) & (i == 0), (rs0m, c - 1))
+            when((c > 1) & (i == 1), (z_done, c - 2))
+            return 0
+
+        def part(i, _):
+            gradient(c, i)
+            when((c == 0) & (i == 0), (ag1m, 2))
+            when((c > 0) & (i == 0), (rs0e, c - 1), (rsd1s, c - 1))
+            return 0
+
+        lax.fori_loop(0, 2, pair, 0)
+        lax.fori_loop(0, 2, part, 0)
         rs0s(c)
-        when(c > 0, (rs1e, c - 1), (z_send, c - 1))
 
     each(work)
     last = CH - 1
+    rsd1e(last - 1)
+    z_send(last - 1)
+    for k in range(2):
+        peer_copy(k).wait_recv()
+    finish(0)
     rs0m(last)
     z_done(last - 1)
+    finish(1)
     rs0e(last)
-    rs1s(last)
-    for distance in (1, 2):
-        for k in range(2):
-            peer_copy(distance, k).wait_recv()
-    for c in range(last - 1):
-        finish(c)
-    rs1m(last)
+    rsd1s(last)
     finish(last - 1)
-    rs1e(last)
+    rsd1e(last)
     z_send(last)
     z_done(last)
     finish(last)
@@ -476,46 +558,62 @@
             rc(b["piece"].at[c, d], b["pin"].at[c, my_slot], c, M_QUAD + k, where).wait_send()
         for half in range(2):
             for phase in range(2):
-                for k in range(4):
-                    ag_copy(c, half, phase, k, up(axis_of(half, phase)["me"], (0, 0, 3, 1)[k])).wait_send()
-                for k in range(6):
-                    rs_copy(c, half, phase, k).wait_send()
+                me = axis_of(half, phase)["me"]
+                if phase == 0:
+                    for k in range(3):
+                        agd_copy(c, half, phase, k, me).wait_send()
+                    for k in range(6):
+                        rs_copy(c, half, phase, k).wait_send()
+                else:
+                    for k in range(4):
+                        ag_copy(c, half, phase, k, up(me, (0, 0, 3, 1)[k])).wait_send()
+                    for k in range(3):
+                        for part in ("p", "q"):
+                            rsd_copy(c, half, phase, k, part).wait_send()
         z_copy(c).wait_send()
         fix_copy(c, core).wait_send()
-        for distance in (1, 2):
-            for rel in (0, 1):
-                gossip_copy(c, distance, rel, core).wait_send()
+        for rel in (0, 1):
+            gossip_copy(c, rel, core).wait_send()
 
     each(drain)
     for k in range(3):
         exchange(k, core).wait_send()
-    for distance in (1, 2):
-        for k in range(2):
-            peer_copy(distance, k).wait_send()
-
-
-def shards(step_index, tokens, queries, cotangent, params, momentum):
-    cos, sin = rope_tables()
+    for i in range(2):
+        for k in range(BLOCKS):
+            out_copy(i, k).wait()
+    for k in range(2):
+        peer_copy(k).wait_send()
+
+
+def step_kernel(distance):
     anywhere = pl.BlockSpec(memory_space=pl.ANY)
-    vmem = pl.BlockSpec(memory_space=pltpu.VMEM)
-    sum_p, sum_m = pl.pallas_call(
-        kernel,
-        out_shape=[jax.ShapeDtypeStruct((LINES, 128), F32)] * 2,
-        in_specs=[pl.BlockSpec(memory_space=pltpu.SMEM)] + [anywhere] * 5 + [vmem] * 2,
-        out_specs=[vmem, vmem],
+    return pl.pallas_call(
+        functools.partial(kernel, distance),
+        out_shape=[jax.ShapeDtypeStruct((OWN, BLOCKS, 128), F32)] * 2,
+        in_specs=[pl.BlockSpec(memory_space=pltpu.SMEM)] + [anywhere] * 7,
+        out_specs=[anywhere, anywhere],
         scratch_shapes=[pltpu.VMEM(shape, dtype) for shape, dtype in SCRATCH.values()]
         + [
             pltpu.SemaphoreType.DMA((CH, M_ALL)),
             pltpu.SemaphoreType.DMA((CH, M_ALL)),
-            pltpu.SemaphoreType.DMA((7,)),
-            pltpu.SemaphoreType.DMA((7,)),
             pltpu.SemaphoreType.DMA((5,)),
+            pltpu.SemaphoreType.DMA((5,)),
+            pltpu.SemaphoreType.DMA((5,)),
+            pltpu.SemaphoreType.DMA((2, BLOCKS)),
+            pltpu.SemaphoreType.DMA((2, BLOCKS)),
         ],
         compiler_params=pltpu.CompilerParams(
-            collective_id=0, has_side_effects=True, vmem_limit_bytes=60 * 2**20),
+            collective_id=distance, has_side_effects=True, vmem_limit_bytes=60 * 2**20),
         cost_estimate=pl.CostEstimate(flops=13 * 10**9, bytes_accessed=10**7, transcendentals=4 * 10**6),
-    )(step_index, tokens, queries, cotangent, params.reshape(LINES, 128), momentum.reshape(LINES, 128),
-      jnp.asarray(cos), jnp.asarray(sin))
+    )
+
+
+def shards(step_index, tokens, queries, cotangent, params, momentum):
+    cos, sin = rope_tables()
+    operands = (step_index, tokens, queries, cotangent, params.reshape(OWN, BLOCKS, 128),
+                momentum.reshape(OWN, BLOCKS, 128), jnp.asarray(cos), jnp.asarray(sin))
+    sum_p, sum_m = lax.cond(
+        (step_index[0] & 1) == 0, *[lambda *xs, d=d: tuple(step_kernel(d)(*xs)) for d in (1, 2)], *operands)
     return (0.5 * sum_p).reshape(1, OWN, WIDE), (0.5 * sum_m).reshape(1, OWN, WIDE)
 
 

time: 124 us -> 103 us (0.83)
  Pallas kernels: 121 us -> 101 us
    pallas_call x1, Pallas kernels: 121 us -> 101 us  [shards(): step_kernel(d)(*xs)]
where the time goes in v3:
time: 103 us
  Pallas kernels  101 us (98%)
  between operations  1.29 us (1%)
    pallas_call x1, Pallas kernels, shards(): step_kernel(d)(*xs)  101 us

profile of v3, /device:TPU:1, one launch (start us, length us, event | category | flops | bytes accessed | tf_op | source)
XLA Modules:
  0.0 103.3 jit_solution(14467644199168828217)
XLA Ops:
  1.3 101.1 %conditional.1 = ((f32[36,16,128]{2,1,0:T(8,128)S(1)}, f32[36,16,128]{2,1,0:T(8,128)S(1)})) conditional(s32[]{:T(128)} %bitcast, (s32[1]{0:T(128)}, bf16[1,512,2304]{2,1,0:T(8,128)(2,1)}, bf16[1,512,2048]{2,1,0:T(8,128)(2,1)}, bf16[1,512,2048]{2,1,0:T(8,128)(2,1)}, f32[36,16,128]{2,1,0:T(8,128)}, /*index=5*/f32[36,16,128]{2,1,0:T(8,128)}, ...), branch_computations={%region_0.0_spmd, %region_1.0_spmd} | conditional | flops 12999999488 | bytes 10000008 | solution.py:615
  1.5 100.9 %branch_1_fun.1 = (f32[36,16,128]{2,1,0:T(8,128)S(1)}, f32[36,16,128]{2,1,0:T(8,128)S(1)}) custom-call(s32[1]{0:T(128)} %get-tuple-element.40.step_ref, bf16[1,512,2304]{2,1,0:T(8,128)(2,1)} %get-tuple-element.41.tok_h, bf16[1,512,2048]{2,1,0:T(8,128)(2,1)} %get-tuple-element.42.q_h, bf16[1,512,2048]{2,1,0:T(8,128)(2,1)} %get-tuple-element.43.cot_h, ...), custom_call_target="tpu_custom_call" | custom-call | flops 12999999488 | bytes 10000000 | tf_op jit(solution)/shard_map/cond/branch_1_fun/pallas_call | solution.py:616
  102.4 0.9 broadcast_multiply_fusion

commit v4 on v3

--- a/solution.py
+++ b/solution.py
@@ -503,6 +503,9 @@
     transpose_rows(other * 2)
     agd0e(2)
     ag1s(2)
+    ag1m(1)
+    agd0e(3)
+    ag1s(3)
     transpose_rows(other * 2 + 1)
     for k in (1, 2):
         exchange(k, other).wait_recv()
@@ -513,76 +516,93 @@
         ag1e(c)
 
         project(c)
-        when(c == 0, (ag1m, 1))
-        when(c > 1, (rsd1e, c - 2), (z_send, c - 2))
+        when(c == 1, (ag1m, 3))
+        when(c > 1, (rs0e, c - 2), (rsd1s, c - 2))
 
         def pair(i, _):
             attend(c, 2 * i)
             attend(c, 2 * i + 1)
-            when((c == 0) & (i == 0), (agd0e, 3), (ag1s, 3))
-            when((c == 1) & (i == 0), (ag1m, 3))
-            when((c > 0) & (i == 0), (rs0m, c - 1))
-            when((c > 1) & (i == 1), (z_done, c - 2))
+            when((c == 0) & (i == 0), (ag1m, 2))
+            when((c == CH - 1) & (i == 0), (z_done, 0))
+            when((c > 0) & (i == 1), (rs0m, c - 1))
             return 0
 
         def part(i, _):
             gradient(c, i)
-            when((c == 0) & (i == 0), (ag1m, 2))
-            when((c > 0) & (i == 0), (rs0e, c - 1), (rsd1s, c - 1))
+            when((c > 1) & (i == 0), (rsd1e, c - 2), (z_send, c - 2))
             return 0
 
         lax.fori_loop(0, 2, pair, 0)
         lax.fori_loop(0, 2, part, 0)
         rs0s(c)
 
+    def drain_gather(c):
+        for k, (where, _, d) in enumerate(quad):
+            rc(b["piece"].at[c, d], b["pin"].at[c, my_slot], c, M_QUAD + k, where).wait_send()
+        for half in range(2):
+            me = axis_of(half, 0)["me"]
+            for k in range(3):
+                agd_copy(c, half, 0, k, me).wait_send()
+            me = axis_of(half, 1)["me"]
+            for k in range(4):
+                ag_copy(c, half, 1, k, up(me, (0, 0, 3, 1)[k])).wait_send()
+
+    def drain_wide(c):
+        for half in range(2):
+            for k in range(6):
+                rs_copy(c, half, 0, k).wait_send()
+
+    def drain_narrow(c):
+        for half in range(2):
+            for k in range(3):
+                for part in ("p", "q"):
+                    rsd_copy(c, half, 1, k, part).wait_send()
+
+    def drain_end(c):
+        z_copy(c).wait_send()
+        fix_copy(c, core).wait_send()
+        for rel in (0, 1):
+            gossip_copy(c, rel, core).wait_send()
+        for i in range(2):
+            for k in (0, 4, 8, 12):
+                out_copy(i, k + c).wait()
+
     each(work)
     last = CH - 1
+    each(drain_gather)
+    rs0e(last - 1)
+    rsd1s(last - 1)
+    rs0m(last)
+    z_done(last - 2)
+    drain_wide(0)
     rsd1e(last - 1)
     z_send(last - 1)
     for k in range(2):
         peer_copy(k).wait_recv()
     finish(0)
-    rs0m(last)
-    z_done(last - 1)
-    finish(1)
     rs0e(last)
     rsd1s(last)
-    finish(last - 1)
+    finish(1)
+    drain_wide(1)
+    drain_wide(2)
+    z_done(last - 1)
+    drain_narrow(0)
+    drain_narrow(1)
     rsd1e(last)
     z_send(last)
-    z_done(last)
-    finish(last)
-
-    def drain(c):
-        for k, (where, _, d) in enumerate(quad):
-            rc(b["piece"].at[c, d], b["pin"].at[c, my_slot], c, M_QUAD + k, where).wait_send()
-        for half in range(2):
-            for phase in range(2):
-                me = axis_of(half, phase)["me"]
-                if phase == 0:
-                    for k in range(3):
-                        agd_copy(c, half, phase, k, me).wait_send()
-                    for k in range(6):
-                        rs_copy(c, half, phase, k).wait_send()
-                else:
-                    for k in range(4):
-                        ag_copy(c, half, phase, k, up(me, (0, 0, 3, 1)[k])).wait_send()
-                    for k in range(3):
-                        for part in ("p", "q"):
-                            rsd_copy(c, half, phase, k, part).wait_send()
-        z_copy(c).wait_send()
-        fix_copy(c, core).wait_send()
-        for rel in (0, 1):
-            gossip_copy(c, rel, core).wait_send()
-
-    each(drain)
+    finish(last - 1)
+    drain_wide(3)
+    drain_narrow(2)
     for k in range(3):
         exchange(k, core).wait_send()
-    for i in range(2):
-        for k in range(BLOCKS):
-            out_copy(i, k).wait()
     for k in range(2):
         peer_copy(k).wait_send()
+    z_done(last)
+    drain_narrow(3)
+    for c in range(last):
+        drain_end(c)
+    finish(last)
+    drain_end(last)
 
 
 def step_kernel(distance):

time: 103 us -> 93.7 us (0.910)
  Pallas kernels: 101 us -> 91.6 us
    pallas_call x1, Pallas kernels: 101 us -> 91.6 us  [shards(): step_kernel(d)(*xs)]
where the time goes in v4:
time: 93.7 us; the launch traced here: 93.9 us
  Pallas kernels  91.6 us (98%)
  between operations  1.29 us (1%)
    pallas_call x1, Pallas kernels, shards(): step_kernel(d)(*xs)  91.6 us

profile of v4, /device:TPU:1, one launch (start us, length us, event | category | flops | bytes accessed | tf_op | source)
XLA Modules:
  0.0 93.9 jit_solution(9534382453248373869)
XLA Ops:
  1.3 91.8 %conditional.1 = ((f32[36,16,128]{2,1,0:T(8,128)S(1)}, f32[36,16,128]{2,1,0:T(8,128)S(1)})) conditional(s32[]{:T(128)} %bitcast, (s32[1]{0:T(128)}, bf16[1,512,2304]{2,1,0:T(8,128)(2,1)}, bf16[1,512,2048]{2,1,0:T(8,128)(2,1)}, bf16[1,512,2048]{2,1,0:T(8,128)(2,1)}, f32[36,16,128]{2,1,0:T(8,128)}, /*index=5*/f32[36,16,128]{2,1,0:T(8,128)}, ...), branch_computations={%region_0.0_spmd, %region_1.0_spmd} | conditional | flops 12999999488 | bytes 10000008 | solution.py:635
  1.3 91.6 %branch_0_fun.1 = (f32[36,16,128]{2,1,0:T(8,128)S(1)}, f32[36,16,128]{2,1,0:T(8,128)S(1)}) custom-call(s32[1]{0:T(128)} %get-tuple-element.32.step_ref, bf16[1,512,2304]{2,1,0:T(8,128)(2,1)} %get-tuple-element.33.tok_h, bf16[1,512,2048]{2,1,0:T(8,128)(2,1)} %get-tuple-element.34.q_h, bf16[1,512,2048]{2,1,0:T(8,128)(2,1)} %get-tuple-element.35.cot_h, ...), custom_call_target="tpu_custom_call" | custom-call | flops 12999999488 | bytes 10000000 | tf_op jit(solution)/shard_map/cond/branch_0_fun/pallas_call | solution.py:636
  93.1 0.9 broadcast_multiply_fusion

commit v5 on v4

--- a/solution.py
+++ b/solution.py
@@ -355,11 +355,11 @@
         pad = jnp.zeros((8, 128), F32)
         b["gb"][c, 0] = jnp.concatenate([first, pad], axis=0).astype(BF16)
         b["gb"][c, 1] = jnp.concatenate([last, pad], axis=0).astype(BF16)
-        b["fs"][c] = jnp.where(core == 0, last, first)
-        b["gx"][c, core] = jnp.where(core == 0, first, last)
         for rel in (0, 1):
             gossip_copy(c, rel, core).start()
+        b["fs"][c] = jnp.where(core == 0, last, first)
         fix_copy(c, core).start()
+        b["gx"][c, core] = jnp.where(core == 0, first, last)
 
     t = step_ref[0]
     learn_now = LEARN_RATE * (t.astype(F32) + 1.0) / WARM_SPAN
@@ -569,29 +569,26 @@
 
     each(work)
     last = CH - 1
-    each(drain_gather)
     rs0e(last - 1)
     rsd1s(last - 1)
     rs0m(last)
     z_done(last - 2)
-    drain_wide(0)
     rsd1e(last - 1)
     z_send(last - 1)
+    rs0e(last)
+    rsd1s(last)
     for k in range(2):
         peer_copy(k).wait_recv()
     finish(0)
-    rs0e(last)
-    rsd1s(last)
+    z_done(last - 1)
+    rsd1e(last)
+    z_send(last)
     finish(1)
-    drain_wide(1)
-    drain_wide(2)
-    z_done(last - 1)
+    each(drain_gather)
+    each(drain_wide)
     drain_narrow(0)
     drain_narrow(1)
-    rsd1e(last)
-    z_send(last)
     finish(last - 1)
-    drain_wide(3)
     drain_narrow(2)
     for k in range(3):
         exchange(k, core).wait_send()

time: 93.7 us -> 93.3 us (level)
  no operation moved by 1% of the time
where the time goes in v5:
time: 93.3 us; the launch traced here: 93.2 us
  Pallas kernels  90.9 us (97%)
  between operations  1.29 us (1%)
    pallas_call x1, Pallas kernels, shards(): step_kernel(d)(*xs)  90.9 us

profile of v5, /device:TPU:1, one launch (start us, length us, event | category | flops | bytes accessed | tf_op | source)
XLA Modules:
  0.0 93.2 jit_solution(2149112364040444988)
XLA Ops:
  1.3 91.1 %conditional.1 = ((f32[36,16,128]{2,1,0:T(8,128)S(1)}, f32[36,16,128]{2,1,0:T(8,128)S(1)})) conditional(s32[]{:T(128)} %bitcast, (s32[1]{0:T(128)}, bf16[1,512,2304]{2,1,0:T(8,128)(2,1)}, bf16[1,512,2048]{2,1,0:T(8,128)(2,1)}, bf16[1,512,2048]{2,1,0:T(8,128)(2,1)}, f32[36,16,128]{2,1,0:T(8,128)}, /*index=5*/f32[36,16,128]{2,1,0:T(8,128)}, ...), branch_computations={%region_0.0_spmd, %region_1.0_spmd} | conditional | flops 12999999488 | bytes 10000008 | solution.py:632
  1.5 90.9 %branch_1_fun.1 = (f32[36,16,128]{2,1,0:T(8,128)S(1)}, f32[36,16,128]{2,1,0:T(8,128)S(1)}) custom-call(s32[1]{0:T(128)} %get-tuple-element.40.step_ref, bf16[1,512,2304]{2,1,0:T(8,128)(2,1)} %get-tuple-element.41.tok_h, bf16[1,512,2048]{2,1,0:T(8,128)(2,1)} %get-tuple-element.42.q_h, bf16[1,512,2048]{2,1,0:T(8,128)(2,1)} %get-tuple-element.43.cot_h, ...), custom_call_target="tpu_custom_call" | custom-call | flops 12999999488 | bytes 10000000 | tf_op jit(solution)/shard_map/cond/branch_1_fun/pallas_call | solution.py:633
  92.4 0.9 broadcast_multiply_fusion
